TPU v7x, 32 devices: a whole 2x2x4 slice. The times are simulated.
32 devices in a mesh: replica: 8 (over z, y), shard: 4 (over x, core).
Axes of the slice: x: 2, y: 2, z: 4, core: 2. Of those that a mesh axis runs over, the one named last changes fastest.
Arguments:
- tokens: bfloat16 [32768, 1024], P(('replica', 'shard')), may hold values from -6 to 6
- lengths: int32 [32, 3], P(('replica', 'shard')), may hold values from 1 to 512, 1024 in all within a row
- attention_gain: bfloat16 [1024], P('shard'), may hold values from 0.5 to 1.5
- query_weight: bfloat16 [1024, 2048], P('shard'), may hold values from -0.1875 to 0.1875
- key_weight: bfloat16 [1024, 1024], P('shard'), may hold values from -0.1875 to 0.1875
- value_weight: bfloat16 [1024, 1024], P('shard'), may hold values from -0.1875 to 0.1875
- query_gain: bfloat16 [128], P('shard'), may hold values from 0.5 to 1.5
- key_gain: bfloat16 [128], P('shard'), may hold values from 0.5 to 1.5
- output_weight: bfloat16 [2048, 1024], P('shard'), may hold values from -1 to 1
- feedforward_gain: bfloat16 [1024], P('shard'), may hold values from 0.5 to 1.5
- gate_weight: bfloat16 [1024, 3072], P('shard'), may hold values from -0.1875 to 0.1875
- up_weight: bfloat16 [1024, 3072], P('shard'), may hold values from -0.1875 to 0.1875
- down_weight: bfloat16 [3072, 1024], P('shard'), may hold values from -0.109375 to 0.109375
- cotangent: bfloat16 [32768, 1024], P(('replica', 'shard')), may hold values from -6 to 6
Outputs:
- mixed: bfloat16 [32768, 1024], P(('replica', 'shard'))
- grad_tokens: float32 [32768, 1024], P(('replica', 'shard'))
- grad_attention_gain: float32 [1024], P('shard')
- grad_query_weight: float32 [1024, 2048], P('shard')
- grad_key_weight: float32 [1024, 1024], P('shard')
- grad_value_weight: float32 [1024, 1024], P('shard')
- grad_query_gain: float32 [128], P('shard')
- grad_key_gain: float32 [128], P('shard')
- grad_output_weight: float32 [2048, 1024], P('shard')
- grad_feedforward_gain: float32 [1024], P('shard')
- grad_gate_weight: float32 [1024, 3072], P('shard')
- grad_up_weight: float32 [1024, 3072], P('shard')
- grad_down_weight: float32 [3072, 1024], P('shard')
Inputs may be any that keep to these rules, and one draw needn't show every extreme that they name: Each row holds 3 document lengths that sum to 1024; the longest of each row is exactly 512.
All inputs are finite; a program needn't handle non-finite values.
Results may differ from a plain program's by a relative error of at most 0.02.
Values may be sent and summed in bfloat16 or wider, within the bound.
A program may use at most 384 MiB of HBM per device.

v0:
```python
import jax
import jax.numpy as jnp
from jax import lax
from jax.sharding import PartitionSpec as P

H = 16
KV = 8
HD = 128
SEQ_LEN = 1024


norm_epsilon = 1e-06
rotary_base = 1000000.0
masked_score = -1e30


def doc_layout(lengths, seq_length):
    bounds = jnp.cumsum(lengths, axis=-1)
    places = lax.broadcasted_iota(jnp.int32, (seq_length,), 0)
    passed = (places[None, :, None] >= bounds[:, None, :]).astype(jnp.int32)
    segment = jnp.sum(passed, axis=-1)
    begins = jnp.sum(passed * lengths[:, None, :], axis=-1)
    return (segment, places[None, :] - begins)


def rotary_tables(position, head_size):
    halves = jnp.arange(head_size // 2, dtype=jnp.float32)
    frequency = rotary_base ** (-(2.0 / head_size) * halves)
    angles = position.astype(jnp.float32)[..., None] * frequency
    cosine = jnp.cos(angles)
    sine = jnp.sin(angles)
    return (jnp.concatenate([cosine, cosine], -1), jnp.concatenate([sine, sine], -1))


def rotate(vector, cosine, sine):
    middle = vector.shape[-1] // 2
    turned = jnp.concatenate([-vector[..., middle:], vector[..., :middle]], -1)
    return vector * cosine + turned * sine


def unrotate(gradient, cosine, sine):
    middle = gradient.shape[-1] // 2
    weighted = gradient * sine
    turned = jnp.concatenate([weighted[..., middle:], -weighted[..., :middle]], -1)
    return gradient * cosine + turned


def norm_forward(value, gain):
    factor = lax.rsqrt(jnp.mean(value * value, axis=-1, keepdims=True) + norm_epsilon)
    return (value * factor * gain, factor)


def norm_backward(value, factor, gain, gradient):
    scaled = gradient * gain
    inner = jnp.mean(scaled * value, axis=-1, keepdims=True)
    return (factor * (scaled - value * factor * factor * inner), gradient * value * factor)


def across_rows(left, right):
    return lax.dot_general(
        left, right, (((0,), (0,)), ((), ())), preferred_element_type=jnp.float32
    )


def against_rows(left, right):
    return lax.dot_general(
        left, right, (((1,), (1,)), ((), ())), preferred_element_type=jnp.float32
    )


def block_scores(query_block, key_block, segment, start_row, end_row):
    width_scale = HD ** (-0.5)
    raw = (
        jnp.einsum("nqgrd,nkgd->ngrqk", query_block, key_block, preferred_element_type=jnp.float32)
        * width_scale
    )
    row_ids = start_row + lax.broadcasted_iota(jnp.int32, (end_row - start_row, end_row), 0)
    column_ids = lax.broadcasted_iota(jnp.int32, (end_row - start_row, end_row), 1)
    allowed = (segment[:, start_row:end_row, None] == segment[:, None, :end_row]) & (
        column_ids <= row_ids
    )[None]
    return jnp.where(allowed[:, None, None], raw, masked_score)


def attention_forward(queries, keys, values, segment, block_rows):
    seq_length = queries.shape[1]
    outputs = []
    totals = []
    for start_row in range(0, seq_length, block_rows):
        end_row = start_row + block_rows
        scores = block_scores(
            queries[:, start_row:end_row], keys[:, :end_row], segment, start_row, end_row
        )
        peak = jnp.max(scores, axis=-1, keepdims=True)
        weights = jnp.exp(scores - peak)
        weight_total = jnp.sum(weights, axis=-1, keepdims=True)
        probs = weights / weight_total
        totals.append(peak + jnp.log(weight_total))
        outputs.append(
            jnp.einsum(
                "ngrqk,nkgd->nqgrd",
                probs.astype(jnp.bfloat16),
                values[:, :end_row],
                preferred_element_type=jnp.float32,
            )
        )
    return (jnp.concatenate(outputs, 1), jnp.concatenate(totals, 3))


def attention_backward(queries, keys, values, segment, totals, grad_out, block_rows):
    seq_length = queries.shape[1]
    width_scale = HD ** (-0.5)
    grad_queries = []
    grad_keys = jnp.zeros(keys.shape, jnp.float32)
    grad_values = jnp.zeros(values.shape, jnp.float32)
    for start_row in range(0, seq_length, block_rows):
        end_row = start_row + block_rows
        scores = block_scores(
            queries[:, start_row:end_row], keys[:, :end_row], segment, start_row, end_row
        )
        probs = jnp.exp(scores - totals[:, :, :, start_row:end_row])
        grad_block = grad_out[:, start_row:end_row]
        grad_probs = jnp.einsum(
            "nqgrd,nkgd->ngrqk", grad_block, values[:, :end_row], preferred_element_type=jnp.float32
        )
        carried = jnp.sum(probs * grad_probs, axis=-1, keepdims=True)
        grad_scores = (probs * (grad_probs - carried)).astype(jnp.bfloat16)
        grad_queries.append(
            jnp.einsum(
                "ngrqk,nkgd->nqgrd",
                grad_scores,
                keys[:, :end_row],
                preferred_element_type=jnp.float32,
            )
            * width_scale
        )
        key_part = (
            jnp.einsum(
                "ngrqk,nqgrd->nkgd",
                grad_scores,
                queries[:, start_row:end_row],
                preferred_element_type=jnp.float32,
            )
            * width_scale
        )
        value_part = jnp.einsum(
            "ngrqk,nqgrd->nkgd",
            probs.astype(jnp.bfloat16),
            grad_block,
            preferred_element_type=jnp.float32,
        )
        padding = ((0, 0), (0, seq_length - end_row), (0, 0), (0, 0))
        grad_keys = grad_keys + jnp.pad(key_part, padding)
        grad_values = grad_values + jnp.pad(value_part, padding)
    return (jnp.concatenate(grad_queries, 1), grad_keys, grad_values)


def shards(
    tokens,
    lengths,
    attention_gain,
    query_weight,
    key_weight,
    value_weight,
    query_gain,
    key_gain,
    output_weight,
    feedforward_gain,
    gate_weight,
    up_weight,
    down_weight,
    cotangent,
):
    attn_full = (
        lax.all_gather(attention_gain, "shard", axis=0, tiled=True),
        lax.all_gather(query_weight, "shard", axis=0, tiled=True),
        lax.all_gather(key_weight, "shard", axis=0, tiled=True),
        lax.all_gather(value_weight, "shard", axis=0, tiled=True),
        lax.all_gather(query_gain, "shard", axis=0, tiled=True),
        lax.all_gather(key_gain, "shard", axis=0, tiled=True),
        lax.all_gather(output_weight, "shard", axis=0, tiled=True),
    )
    mlp_full = (
        lax.all_gather(feedforward_gain, "shard", axis=0, tiled=True),
        lax.all_gather(gate_weight, "shard", axis=0, tiled=True),
        lax.all_gather(up_weight, "shard", axis=0, tiled=True),
        lax.all_gather(down_weight, "shard", axis=0, tiled=True),
    )
    gain_one, w_query, w_key, w_value, gain_query, gain_key, w_output = attn_full
    gain_two, w_gate, w_up, w_down = mlp_full
    local_seqs = lengths.shape[0]
    row_total = tokens.shape[0]
    group_heads = H // KV
    block_rows = min(512, SEQ_LEN)
    segment, position = doc_layout(lengths, SEQ_LEN)
    cosine, sine = rotary_tables(position, HD)
    cosine = cosine[:, :, None, :]
    sine = sine[:, :, None, :]
    inputs = tokens.astype(jnp.float32)
    normed, factor_one = norm_forward(inputs, gain_one.astype(jnp.float32))
    acts = normed.astype(jnp.bfloat16)
    query_raw = jnp.dot(acts, w_query, preferred_element_type=jnp.float32).reshape(
        local_seqs, SEQ_LEN, H, HD
    )
    key_raw = jnp.dot(acts, w_key, preferred_element_type=jnp.float32).reshape(
        local_seqs, SEQ_LEN, KV, HD
    )
    values = (
        jnp.dot(acts, w_value, preferred_element_type=jnp.float32)
        .astype(jnp.bfloat16)
        .reshape(local_seqs, SEQ_LEN, KV, HD)
    )
    query_normed, query_factor = norm_forward(query_raw, gain_query.astype(jnp.float32))
    key_normed, key_factor = norm_forward(key_raw, gain_key.astype(jnp.float32))
    queries = (
        rotate(query_normed, cosine, sine)
        .astype(jnp.bfloat16)
        .reshape(local_seqs, SEQ_LEN, KV, group_heads, HD)
    )
    keys = rotate(key_normed, cosine, sine).astype(jnp.bfloat16)
    attended, totals = attention_forward(queries, keys, values, segment, block_rows)
    attended_low = attended.reshape(row_total, H * HD).astype(jnp.bfloat16)
    middle = inputs + jnp.dot(attended_low, w_output, preferred_element_type=jnp.float32)
    normed_two, factor_two = norm_forward(middle, gain_two.astype(jnp.float32))
    acts_two = normed_two.astype(jnp.bfloat16)
    gate_value = jnp.dot(acts_two, w_gate, preferred_element_type=jnp.float32)
    up_value = jnp.dot(acts_two, w_up, preferred_element_type=jnp.float32)
    sigmoid_gate = jax.nn.sigmoid(gate_value)
    hidden = (gate_value * sigmoid_gate * up_value).astype(jnp.bfloat16)
    mixed = (middle + jnp.dot(hidden, w_down, preferred_element_type=jnp.float32)).astype(
        jnp.bfloat16
    )
    gain_two, w_gate, w_up, w_down = (
        lax.all_gather(feedforward_gain, "shard", axis=0, tiled=True),
        lax.all_gather(gate_weight, "shard", axis=0, tiled=True),
        lax.all_gather(up_weight, "shard", axis=0, tiled=True),
        lax.all_gather(down_weight, "shard", axis=0, tiled=True),
    )
    grad_top = cotangent.astype(jnp.float32)
    grad_branch = grad_top.astype(jnp.bfloat16)
    grad_wdown = across_rows(hidden, grad_branch)
    grad_hidden = against_rows(grad_branch, w_down)
    grad_gate = (
        grad_hidden * up_value * sigmoid_gate * (1.0 + gate_value * (1.0 - sigmoid_gate))
    ).astype(jnp.bfloat16)
    grad_up = (grad_hidden * gate_value * sigmoid_gate).astype(jnp.bfloat16)
    grad_wgate = across_rows(acts_two, grad_gate)
    grad_wup = across_rows(acts_two, grad_up)
    grad_acts_two = against_rows(grad_gate, w_gate) + against_rows(grad_up, w_up)
    grad_norm_two, gain_terms_two = norm_backward(
        middle, factor_two, gain_two.astype(jnp.float32), grad_acts_two
    )
    grad_gain_two = jnp.sum(gain_terms_two, axis=0)
    mlp_owned = (
        lax.psum_scatter(
            grad_gain_two.astype(jnp.bfloat16), "shard", scatter_dimension=0, tiled=True
        ).astype(jnp.float32),
        lax.psum_scatter(
            grad_wgate.astype(jnp.bfloat16), "shard", scatter_dimension=0, tiled=True
        ).astype(jnp.float32),
        lax.psum_scatter(
            grad_wup.astype(jnp.bfloat16), "shard", scatter_dimension=0, tiled=True
        ).astype(jnp.float32),
        lax.psum_scatter(
            grad_wdown.astype(jnp.bfloat16), "shard", scatter_dimension=0, tiled=True
        ).astype(jnp.float32),
    )
    mlp_summed = (
        lax.psum(mlp_owned[0].astype(jnp.bfloat16), "replica").astype(jnp.float32),
        lax.psum(mlp_owned[1].astype(jnp.bfloat16), "replica").astype(jnp.float32),
        lax.psum(mlp_owned[2].astype(jnp.bfloat16), "replica").astype(jnp.float32),
        lax.psum(mlp_owned[3].astype(jnp.bfloat16), "replica").astype(jnp.float32),
    )
    gain_one, w_query, w_key, w_value, gain_query, gain_key, w_output = (
        lax.all_gather(attention_gain, "shard", axis=0, tiled=True),
        lax.all_gather(query_weight, "shard", axis=0, tiled=True),
        lax.all_gather(key_weight, "shard", axis=0, tiled=True),
        lax.all_gather(value_weight, "shard", axis=0, tiled=True),
        lax.all_gather(query_gain, "shard", axis=0, tiled=True),
        lax.all_gather(key_gain, "shard", axis=0, tiled=True),
        lax.all_gather(output_weight, "shard", axis=0, tiled=True),
    )
    grad_middle = grad_top + grad_norm_two
    grad_attn = grad_middle.astype(jnp.bfloat16)
    grad_woutput = across_rows(attended_low, grad_attn)
    grad_attended = (
        against_rows(grad_attn, w_output)
        .astype(jnp.bfloat16)
        .reshape(local_seqs, SEQ_LEN, KV, group_heads, HD)
    )
    grad_queries, grad_keys, grad_values = attention_backward(
        queries, keys, values, segment, totals, grad_attended, block_rows
    )
    grad_queries = unrotate(grad_queries.reshape(local_seqs, SEQ_LEN, H, HD), cosine, sine)
    grad_keys = unrotate(grad_keys, cosine, sine)
    grad_query_raw, query_terms = norm_backward(
        query_raw, query_factor, gain_query.astype(jnp.float32), grad_queries
    )
    grad_key_raw, key_terms = norm_backward(
        key_raw, key_factor, gain_key.astype(jnp.float32), grad_keys
    )
    grad_gain_query = jnp.sum(query_terms, axis=(0, 1, 2))
    grad_gain_key = jnp.sum(key_terms, axis=(0, 1, 2))
    grad_query = grad_query_raw.reshape(row_total, H * HD).astype(jnp.bfloat16)
    grad_key = grad_key_raw.reshape(row_total, KV * HD).astype(jnp.bfloat16)
    grad_value = grad_values.reshape(row_total, KV * HD).astype(jnp.bfloat16)
    grad_wquery = across_rows(acts, grad_query)
    grad_wkey = across_rows(acts, grad_key)
    grad_wvalue = across_rows(acts, grad_value)
    grad_acts = (
        against_rows(grad_query, w_query)
        + against_rows(grad_key, w_key)
        + against_rows(grad_value, w_value)
    )
    grad_norm_one, gain_terms_one = norm_backward(
        inputs, factor_one, gain_one.astype(jnp.float32), grad_acts
    )
    grad_gain_one = jnp.sum(gain_terms_one, axis=0)
    grad_tokens = grad_middle + grad_norm_one
    attn_owned = (
        lax.psum_scatter(grad_gain_one, "shard", scatter_dimension=0, tiled=True),
        lax.psum_scatter(grad_wquery, "shard", scatter_dimension=0, tiled=True),
        lax.psum_scatter(grad_wkey, "shard", scatter_dimension=0, tiled=True),
        lax.psum_scatter(grad_wvalue, "shard", scatter_dimension=0, tiled=True),
        lax.psum_scatter(grad_gain_query, "shard", scatter_dimension=0, tiled=True),
        lax.psum_scatter(grad_gain_key, "shard", scatter_dimension=0, tiled=True),
        lax.psum_scatter(grad_woutput, "shard", scatter_dimension=0, tiled=True),
    )
    attn_summed = (
        lax.psum(attn_owned[0].astype(jnp.bfloat16), "replica").astype(jnp.float32),
        lax.psum(attn_owned[1].astype(jnp.bfloat16), "replica").astype(jnp.float32),
        lax.psum(attn_owned[2].astype(jnp.bfloat16), "replica").astype(jnp.float32),
        lax.psum(attn_owned[3].astype(jnp.bfloat16), "replica").astype(jnp.float32),
        lax.psum(attn_owned[4].astype(jnp.bfloat16), "replica").astype(jnp.float32),
        lax.psum(attn_owned[5].astype(jnp.bfloat16), "replica").astype(jnp.float32),
        lax.psum(attn_owned[6].astype(jnp.bfloat16), "replica").astype(jnp.float32),
    )
    return (
        mixed,
        grad_tokens,
        attn_summed[0],
        attn_summed[1],
        attn_summed[2],
        attn_summed[3],
        attn_summed[4],
        attn_summed[5],
        attn_summed[6],
        mlp_summed[0],
        mlp_summed[1],
        mlp_summed[2],
        mlp_summed[3],
    )


def solution(mesh):
    return jax.shard_map(
        shards,
        mesh=mesh,
        in_specs=(
            P(("replica", "shard"), None),
            P(("replica", "shard"), None),
            P("shard"),
            P("shard", None),
            P("shard", None),
            P("shard", None),
            P("shard"),
            P("shard"),
            P("shard", None),
            P("shard"),
            P("shard", None),
            P("shard", None),
            P("shard", None),
            P(("replica", "shard"), None),
        ),
        out_specs=(
            P(("replica", "shard"), None),
            P(("replica", "shard"), None),
            P("shard"),
            P("shard", None),
            P("shard", None),
            P("shard", None),
            P("shard"),
            P("shard"),
            P("shard", None),
            P("shard"),
            P("shard", None),
            P("shard", None),
            P("shard", None),
        ),
        check_vma=False,
    )
```

profile of v0, /device:TPU:0, one launch (start us, length us, event | category | flops | bytes accessed | tf_op | source)
XLA Modules:
  0.0 1228.4 jit_solution(3362438323212101654)
XLA Ops:
  114.3 11.8 reshape.920
  154.0 10.8 fusion.28
  164.8 13.6 %fusion.92 = (f32[8,2,512]{2,1,0:T(2,128)S(1)}, f32[1,8,2,512,1024]{3,4,2,1,0:T(8,128)}) fusion(bf16[1024,8,128,1]{2,0,3,1:T(8,128)(2,1)S(1)} %copy-done.11, bf16[1,1024,8,2,128]{4,1,3,2,0:T(8,128)(2,1)S(1)} %fusion.28, pred[512,1024]{0,1:T(8,128)(4,1)S(1)} %copy-done.33), kind=kOutput, calls=%fused_computation.175 | convolution fusion | flops 2172641280 | bytes 38305792 | tf_op jit(solution)/shard_map/nqgrd,nkgd->ngrqk/dot_general | solution.py:74
  178.5 14.7 %fusion.3 = f32[8,2,512]{2,1,0:T(2,128)S(1)} fusion(f32[1,8,2,512,1024]{3,4,2,1,0:T(8,128)} %get-tuple-element.129, f32[8,2,512]{2,1,0:T(2,128)S(1)} %get-tuple-element.128), kind=kLoop, calls=%fused_computation.9 | loop fusion | flops 16769024 | bytes 33619968 | tf_op jit(solution)/shard_map/reduce_sum | solution.py:96
  193.2 15.7 %convert_bitcast_fusion = bf16[1,512,8,2,128]{1,4,3,2,0:T(8,128)(2,1)} fusion(bf16[1024,8,128,1]{0,2,3,1:T(8,128)(2,1)} %bitcast.304, f32[8,2,512]{2,1,0:T(2,128)S(1)} %fusion.3, f32[1,8,2,512,1024]{3,4,2,1,0:T(8,128)} %get-tuple-element.129, f32[8,2,512]{2,1,0:T(2,128)S(1)} %get-tuple-element.128), kind=kOutput, calls=%fused_computation.119 | convolution fusion | flops 2173698048 | bytes 37814272 | tf_op jit(solution)/shard_map/ngrqk,nkgd->nqgrd/dot_general | solution.py:100
  249.8 12.4 %fusion.94 = f32[1024,3072]{1,0:T(8,128)} fusion(bf16[1024,1024]{0,1:T(8,128)(2,1)S(1)} %multiply_convert_fusion.4, bf16[1024,3072]{1,0:T(8,128)(2,1)} %all-gather.18.cloned.1.call-done), kind=kOutput, calls=%fused_computation.177 | convolution fusion | flops 6442450944 | bytes 20971520 | tf_op jit(solution)/shard_map/dot_general | solution.py:226
  262.2 12.3 fusion.95
  274.9 23.2 %multiply_convert_fusion = (bf16[1024,3072]{1,0:T(8,128)(2,1)}, bf16[1024,3072]{1,0:T(8,128)(2,1)}, bf16[1024,3072]{1,0:T(8,128)(2,1)}) fusion(f32[1024,3072]{1,0:T(8,128)} %fusion.94, f32[1024,3072]{1,0:T(8,128)} %fusion.95, bf16[1024,1024]{1,0:T(8,128)(2,1)S(1)} %copy-done.42, bf16[3072,1024]{1,0:T(8,128)(2,1)} %all-gather.22.cloned.1.call-done), kind=kOutput, calls=%fused_computation.29 | convolution fusion | flops 6492782592 | bytes 52428800 | tf_op jit(solution)/shard_map/dot_general | solution.py:66
  298.1 11.0 fusion.96
  341.2 12.6 %fusion.9 = (f32[8,2,512]{2,1,0:T(2,128)S(1)}, f32[8,512,512,2]{2,1,3,0:T(8,128)}) fusion(f32[1,8,2,512,512]{3,4,2,1,0:T(8,128)} %get-tuple-element.131, f32[8,2,512]{2,1,0:T(2,128)S(1)} %bitcast.315, bf16[1,512,8,2,128]{4,3,2,1,0:T(2,128)(2,1)S(1)} %get-tuple-element.116, bf16[1,1024,8,128]{1,3,2,0:T(8,128)(2,1)S(1)} %bitcast.306), kind=kOutput, calls=%fused_computation.17 | convolution fusion | flops 1086316544 | bytes 36765696 | tf_op jit(solution)/shard_map/nqgrd,nkgd->ngrqk/dot_general | solution.py:123
  353.8 12.2 fusion.24
  369.3 22.9 %fusion = (f32[8,2,512]{2,1,0:T(2,128)S(1)}, f32[8,1024,512,2]{2,1,3,0:T(8,128)}) fusion(f32[1,8,2,512,1024]{3,4,2,1,0:T(8,128)} %get-tuple-element.129, f32[8,2,512]{2,1,0:T(2,128)S(1)} %bitcast.312, bf16[1024,8,128,1]{0,2,3,1:T(8,128)(2,1)S(1)} %bitcast.307, bf16[1,512,8,2,128]{4,3,2,1,0:T(2,128)(2,1)S(1)} %get-tuple-element.117), kind=kOutput, calls=%fused_computation.3 | convolution fusion | flops 2172641280 | bytes 71368704 | tf_op jit(solution)/shard_map/nqgrd,nkgd->ngrqk/dot_general | solution.py:123
  392.2 27.8 %fusion.8 = bf16[8,2,512,1024]{2,3,1,0:T(8,128)(2,1)} fusion(f32[8,1024,512,2]{2,1,3,0:T(8,128)} %get-tuple-element.136, f32[1,8,2,512,1024]{3,4,2,1,0:T(8,128)} %get-tuple-element.129, f32[8,2,512]{2,1,0:T(2,128)S(1)} %get-tuple-element.135, f32[8,2,512]{2,1,0:T(2,128)S(1)} %bitcast.313), kind=kLoop, calls=%fused_computation.13 | loop fusion | flops 33554432 | bytes 83951616 | tf_op jit(solution)/shard_map/reshape.73
  420.0 14.1 %fusion.48 = (f32[1,1024,8,128]{3,1,2,0:T(8,128)}, f32[8,128,1024,1]{1,2,3,0:T(8,128)}) fusion(f32[1,512,8,128]{3,1,2,0:T(8,128)S(1)} %fusion.55, f32[1024,128]{1,0:T(8,128)S(1)} %copy-done.28, bf16[8,2,512,1024]{2,3,1,0:T(8,128)(2,1)} %fusion.8, bf16[1,1024,8,2,128]{4,1,3,2,0:T(8,128)(2,1)} %copy-done.9), kind=kOutput, calls=%fused_computation.106 | convolution fusion | flops 2150629376 | bytes 29884416 | tf_op jit(solution)/shard_map/ngrqk,nqgrd->nkgd/dot_general | solution.py:138
  459.3 11.7 fusion.65
  471.0 16.9 %fusion.47 = bf16[1,1024,8,128]{1,3,2,0:T(8,128)(2,1)} fusion(f32[1,512,8,128]{1,3,2,0:T(8,128)} %fusion.65, f32[1,8,2,512,1024]{3,4,2,1,0:T(8,128)} %get-tuple-element.129, f32[8,2,512]{2,1,0:T(2,128)S(1)} %bitcast.314, bf16[1,512,8,2,128]{4,3,2,1,0:T(2,128)(2,1)} %copy-done.13), kind=kOutput, calls=%fused_computation.87 | convolution fusion | flops 2166358016 | bytes 39878656 | tf_op jit(solution)/shard_map/ngrqk,nqgrd->nkgd/dot_general | solution.py:146
  503.2 10.5 multiply_bitcast_fusion
  524.2 11.0 fusion.87
  579.0 22.9 %fusion.26 = (f32[2048]{0:T(1024)S(1)}, bf16[1024,2048]{1,0:T(8,128)(2,1)}) fusion(f32[1024,2048]{1,0:T(8,128)} %fusion.82, f32[128,8,16,128]{3,2,1,0:T(8,128)} %bitcast.296, f32[1024,2048]{1,0:T(8,128)} %copy.224, f32[1024,2048]{1,0:T(8,128)} %copy.282, f32[128,8,16,128]{3,2,1,0:T(8,128)} %bitcast.297, f32[128,8,16,128]{3,2,1,0:T(8,128)} %bitcast.298, ...), kind=kLoop, calls=%fused_computation.43 | loop fusion | flops 25163776 | bytes 54542336 | tf_op jit(solution)/shard_map/reduce_sum | solution.py:302
  611.6 13.0 %fusion.69 = f32[2048,1024]{1,0:T(8,128)} fusion(bf16[1024,2048]{0,1:T(8,128)(2,1)} %bitcast.309, f32[1024,1024]{0,1:T(8,128)} %copy-done.19), kind=kOutput, calls=%fused_computation.132 | convolution fusion | flops 4296015872 | bytes 16777216 | tf_op jit(solution)/shard_map/dot_general | solution.py:60
  624.6 11.7 convolution_convert_fusion.2
  636.4 11.1 convolution_convert_fusion.1
  647.6 11.4 convolution_convert_fusion
  663.3 20.0 %reduce-scatter.8.cloned.1.call-done = f32[256,2048]{1,0:T(8,128)} async-done(((f32[1024,2048]{1,0:T(8,128)}), f32[256,2048]{1,0:T(8,128)}) %reduce-scatter.8.cloned.1.call-update) | async-done | bytes 2097168 | tf_op jit(solution)/shard_map/reduce_scatter | solution.py:322
  686.1 71.8 %reduce-scatter.14.cloned.1.call-done = f32[512,1024]{1,0:T(8,128)} async-done(((f32[2048,1024]{1,0:T(8,128)}), f32[512,1024]{1,0:T(8,128)}) %reduce-scatter.14.cloned.1.call-update) | async-done | bytes 2097168 | tf_op jit(solution)/shard_map/reduce_scatter | solution.py:327
  760.6 58.1 %reduce-scatter.16.cloned.1.call-done = bf16[256,3072]{1,0:T(8,128)(2,1)} async-done(((bf16[1024,3072]{1,0:T(8,128)(2,1)}), bf16[256,3072]{1,0:T(8,128)(2,1)}) %reduce-scatter.16.cloned.1.call-update) | async-done | bytes 1572880 | tf_op jit(solution)/shard_map/reduce_scatter | solution.py:258
  818.7 61.1 %reduce-scatter.18.cloned.1.call-done = bf16[256,3072]{1,0:T(8,128)(2,1)} async-done(((bf16[1024,3072]{1,0:T(8,128)(2,1)}), bf16[256,3072]{1,0:T(8,128)(2,1)}) %reduce-scatter.18.cloned.1.call-update) | async-done | bytes 1572880 | tf_op jit(solution)/shard_map/reduce_scatter | solution.py:261
  879.8 60.8 %reduce-scatter.20.cloned.1.call-done = bf16[768,1024]{1,0:T(8,128)(2,1)} async-done(((bf16[3072,1024]{1,0:T(8,128)(2,1)}), bf16[768,1024]{1,0:T(8,128)(2,1)}) %reduce-scatter.20.cloned.1.call-update) | async-done | bytes 1572880 | tf_op jit(solution)/shard_map/reduce_scatter | solution.py:264
  941.9 12.3 %add_convert_fusion = bf16[1024,1024]{0,1:T(8,128)(2,1)} fusion(f32[1024,1024]{0,1:T(8,128)} %copy-done.17, bf16[1024,3072]{1,0:T(8,128)(2,1)} %get-tuple-element.107, bf16[3072,1024]{1,0:T(8,128)(2,1)} %all-gather.22.cloned.1.call-done), kind=kOutput, calls=%fused_computation.100 | convolution fusion | flops 6444548096 | bytes 18874368 | tf_op jit(solution)/shard_map/dot_general | solution.py:230
  979.4 10.9 all-reduce.8
  996.7 22.4 %all-reduce.9 = (bf16[256]{0:T(256)(128)(2,1)S(1)}, bf16[32]{0:T(256)(128)(2,1)S(1)}, bf16[32]{0:T(256)(128)(2,1)S(1)}, bf16[256]{0:T(256)(128)(2,1)S(1)}) all-reduce(bf16[256]{0:T(256)(128)(2,1)S(1)} %dynamic-slice.13, bf16[32]{0:T(256)(128)(2,1)S(1)} %dynamic-slice.15, ...), channel_id=1, replica_groups=mesh['replica'=8,'shard'=4] {'replica'}, use_global_device_ids=true, to_apply=%region_19.20 | all-reduce | flops 576 | bytes 2304 | tf_op jit(solution)/shard_map/psum | solution.py:330
  1021.3 186.5 %all-reduce.14.cloned.1.call-done = (bf16[256,2048]{1,0:T(8,128)(2,1)}, bf16[256,1024]{1,0:T(8,128)(2,1)}, bf16[256,1024]{1,0:T(8,128)(2,1)}, bf16[512,1024]{1,0...) async-done(((bf16[256,2048]{1,0:T(8,128)(2,1)}, bf16[256,1024]{1,0:T(8,128)(2,1)}, bf16[256,1024]{1,0:T(8,128)(2,1)}, ...) | async-done | bytes 7864336 | tf_op jit(solution)/shard_map/psum | solution.py:331
  (315 shorter events, 372.2 us)
Async XLA Ops:
  7.2 41.1 %all-gather.12.cloned.1.call-start = ((), (), s32[]{:S(2)}) async-start(), calls=%async_computation.8 | async-start | bytes 2621440 | tf_op jit(solution)/shard_map/all_gather | solution.py:177
  7.9 80.9 %all-gather.10.cloned.1.call-start = ((), (), s32[]{:S(2)}) async-start(), calls=%async_computation.7 | async-start | bytes 2621440 | tf_op jit(solution)/shard_map/all_gather | solution.py:178
  8.7 86.6 %all-gather.14.cloned.1.call-start = ((), (), s32[]{:S(2)}) async-start(), calls=%async_computation.9 | async-start | bytes 5242880 | tf_op jit(solution)/shard_map/all_gather | solution.py:176
  9.4 227.4 %all-gather.16.cloned.1.call-start = ((), (), s32[]{:S(2)}) async-start(), calls=%async_computation.10 | async-start | bytes 5242880 | tf_op jit(solution)/shard_map/all_gather | solution.py:181
  10.0 238.5 %all-gather.18.cloned.1.call-start = ((), (), s32[]{:S(2)}) async-start(), calls=%async_computation.11 | async-start | bytes 7864320 | tf_op jit(solution)/shard_map/all_gather | solution.py:185
  10.6 251.6 %all-gather.20.cloned.1.call-start = ((), (), s32[]{:S(2)}) async-start(), calls=%async_computation.12 | async-start | bytes 7864320 | tf_op jit(solution)/shard_map/all_gather | solution.py:186
  11.2 20.3 %copy-start.68 = (s32[1,3]{1,0:T(1,128)S(1)}, s32[1,3]{1,0:T(1,128)}, u32[]{:S(2)}) copy-start(s32[1,3]{1,0:T(1,128)} %param.15) | copy-start | bytes 40
  11.2 263.7 %all-gather.22.cloned.1.call-start = ((), (), s32[]{:S(2)}) async-start(), calls=%async_computation.13 | async-start | bytes 7864320 | tf_op jit(solution)/shard_map/all_gather | solution.py:187
  11.9 647.2 %reduce-scatter.10.cloned.1.call-start = ((), (), s32[]{:S(2)}) async-start(), calls=%async_computation.15 | async-start | bytes 5242880 | tf_op jit(solution)/shard_map/reduce_scatter | solution.py:323
  14.9 221.9 %copy-start.5 = (bf16[1024,1024]{0,1:T(8,128)(2,1)}, bf16[1024,1024]{0,1:T(8,128)(2,1)S(1)}, u32[]{:S(2)}) copy-start(bf16[1024,1024]{0,1:T(8,128)(2,1)S(1)} %copy.194) | copy-start | bytes 6291460
  14.9 21.9 %copy-start.75 = (bf16[256]{0:T(256)(128)(2,1)S(1)}, bf16[256]{0:T(256)(128)(2,1)}, u32[]{:S(2)}) copy-start(bf16[256]{0:T(256)(128)(2,1)} %param.23) | copy-start | bytes 1540
  21.1 74.2 %copy-start.55 = (f32[4,1,256]{2,1,0:T(1,128)}, f32[4,1,256]{2,1,0:T(1,128)S(1)}, u32[]{:S(2)}) copy-start(f32[4,1,256]{2,1,0:T(1,128)S(1)} %convert_element_type.265) | copy-start | bytes 12292
  21.6 73.7 %copy-start.57 = (f32[1024]{0:T(1024)}, f32[1024]{0:T(1024)S(1)}, u32[]{:S(2)}) copy-start(f32[1024]{0:T(1024)S(1)} %add_rsqrt_fusion.3) | copy-start | bytes 12292
  31.4 46.4 %copy-start.63 = (f32[128]{0:T(128)}, f32[128]{0:T(128)S(1)}, u32[]{:S(2)}) copy-start(f32[128]{0:T(128)S(1)} %convert_element_type.216) | copy-start | bytes 1540
  35.9 18.6 %copy-start.21 = (f32[1024,128]{1,0:T(8,128)}, f32[1024,128]{1,0:T(8,128)S(1)}, u32[]{:S(2)}) copy-start(f32[1024,128]{1,0:T(8,128)S(1)} %copy.196) | copy-start | bytes 1572868
  35.9 118.1 %copy-start.61 = (f32[128]{0:T(128)}, f32[128]{0:T(128)S(1)}, u32[]{:S(2)}) copy-start(f32[128]{0:T(128)S(1)} %convert_element_type.219) | copy-start | bytes 1540
  193.1 15.7 %copy-start.24 = (bf16[512,8,128,1]{2,0,3,1:T(8,128)(2,1)S(1)}, bf16[512,8,128,1]{2,0,3,1:T(8,128)(2,1)}, u32[]{:S(2)}) copy-start(bf16[512,8,128,1]{2,0,3,1:T(8,128)(2,1)} %fusion.68) | copy-start | bytes 3145732
  341.2 28.1 %copy-start.13 = (bf16[1,512,8,2,128]{4,3,2,1,0:T(2,128)(2,1)}, bf16[1,512,8,2,128]{4,3,2,1,0:T(2,128)(2,1)S(1)}, u32[]{:S(2)}) copy-start(bf16[1,512,8,2,128]{4,3,2,1,0:T(2,128)(2,1)S(1)} %get-tuple-element.117) | copy-start | bytes 6291460
  369.3 50.7 %copy-start.39 = (f32[1,512,8,128]{3,1,2,0:T(8,128)}, f32[1,512,8,128]{3,1,2,0:T(8,128)S(1)}, u32[]{:S(2)}) copy-start(f32[1,512,8,128]{3,1,2,0:T(8,128)S(1)} %fusion.55) | copy-start | bytes 6291460
  392.2 27.8 %copy-start.28 = (f32[1024,128]{1,0:T(8,128)S(1)}, f32[1024,128]{1,0:T(8,128)}, u32[]{:S(2)}) copy-start(f32[1024,128]{1,0:T(8,128)} %copy.197) | copy-start | bytes 1572868
  459.3 201.9 %reduce-scatter.12.cloned.1.call-start = ((), (), s32[]{:S(2)}) async-start(), calls=%async_computation.16 | async-start | bytes 5242880 | tf_op jit(solution)/shard_map/reduce_scatter | solution.py:324
  493.9 189.5 %reduce-scatter.8.cloned.1.call-start = ((), (), s32[]{:S(2)}) async-start(), calls=%async_computation.14 | async-start | bytes 10485760 | tf_op jit(solution)/shard_map/reduce_scatter | solution.py:322
  513.8 21.5 %slice-start = ((s8[8388608]{0:T(1024)(128)(4,1)}), s8[4194304]{0:T(1024)(128)(4,1)S(1)}, s32[]{:S(2)}) async-start(s8[8388608]{0:T(1024)(128)(4,1)} %bitcast.287), calls=%async_computation.22 | async-start | bytes 8388608
  519.5 15.7 %copy-start = (f32[1,1024,8,2,128]{1,4,3,2,0:T(8,128)}, f32[1,1024,8,2,128]{1,4,3,2,0:T(8,128)S(1)}, u32[]{:S(2)}) copy-start(f32[1,1024,8,2,128]{1,4,3,2,0:T(8,128)S(1)} %pad_maximum_fusion) | copy-start | bytes 25165828
  519.5 15.7 %slice-start.1 = ((s8[8388608]{0:T(1024)(128)(4,1)}), s8[4194304]{0:T(1024)(128)(4,1)S(1)}, s32[]{:S(2)}) async-start(s8[8388608]{0:T(1024)(128)(4,1)} %bitcast.287), calls=%async_computation.23 | async-start | bytes 8388608
  579.0 22.9 %copy-start.7 = (bf16[1024,1024]{0,1:T(8,128)(2,1)S(1)}, bf16[1024,1024]{0,1:T(8,128)(2,1)}, u32[]{:S(2)}) copy-start(bf16[1024,1024]{0,1:T(8,128)(2,1)} %copy-done.5) | copy-start | bytes 6291460
  611.5 146.4 %reduce-scatter.14.cloned.1.call-start = ((), (), s32[]{:S(2)}) async-start(), calls=%async_computation.17 | async-start | bytes 10485760 | tf_op jit(solution)/shard_map/reduce_scatter | solution.py:327
  624.6 194.1 %reduce-scatter.16.cloned.1.call-start = ((), (), s32[]{:S(2)}) async-start(), calls=%async_computation.18 | async-start | bytes 7864320 | tf_op jit(solution)/shard_map/reduce_scatter | solution.py:258
  636.4 243.4 %reduce-scatter.18.cloned.1.call-start = ((), (), s32[]{:S(2)}) async-start(), calls=%async_computation.19 | async-start | bytes 7864320 | tf_op jit(solution)/shard_map/reduce_scatter | solution.py:261
  647.5 293.0 %reduce-scatter.20.cloned.1.call-start = ((), (), s32[]{:S(2)}) async-start(), calls=%async_computation.20 | async-start | bytes 7864320 | tf_op jit(solution)/shard_map/reduce_scatter | solution.py:264
  659.0 548.7 %all-reduce.14.cloned.1.call-start = ((), (), s32[]{:S(2)}) async-start(), calls=%async_computation.21 | async-start | bytes 15728640 | tf_op jit(solution)/shard_map/psum | solution.py:331
  974.0 16.6 %copy-start.67 = (bf16[1024]{0:T(1024)(128)(2,1)S(1)}, bf16[1024]{0:T(1024)(128)(2,1)}, u32[]{:S(2)}) copy-start(bf16[1024]{0:T(1024)(128)(2,1)} %get-tuple-element.78) | copy-start | bytes 6148
  (63 other events, 439.4 us)
Sparse Core Ops, SparseCore 0:
  9.6 25.4 all-gather.11
  36.6 22.5 all-gather.9
  60.8 34.4 all-gather.13
  96.7 34.4 all-gather.15
  132.6 46.3 all-gather.17
  180.5 46.3 all-gather.19
  228.4 46.3 all-gather.21
  459.4 44.5 reduce-scatter.9
  506.7 44.4 reduce-scatter.11
  611.7 71.6 reduce-scatter.7
  686.1 71.7 reduce-scatter.13
  760.3 58.3 reduce-scatter.15
  821.4 58.3 reduce-scatter.17
  882.2 58.3 reduce-scatter.19
  947.8 259.9 all-reduce.13
where the time goes:
time: 1230 us
  waiting for transfers between devices  464 us (38%)
  matrix products  343 us (28%)
  other arithmetic  214 us (17%)
  local copies, waits for them, and re-layouts  130 us (11%)
  blocking collectives  59.1 us (5%)
  between operations  17.1 us (1%)
    psum x1, waiting for transfers between devices, shards(): lax.psum(attn_owned[1].astype(jnp.bfloat16), 'replica').astype(jnp.float32)  186 us
    reduce_scatter x1, waiting for transfers between devices, shards(): lax.psum_scatter(grad_woutput, 'shard', scatter_dimension=0, tiled=True)  71.8 us
    dot_general x7, matrix products, across_rows(): lax.dot_general(left, right, (((0,), (0,)), ((), ())), preferred_element_...  68.6 us
    dot_general x7, matrix products, against_rows(): lax.dot_general(left, right, (((1,), (1,)), ((), ())), preferred_element_...  63 us
    reduce_scatter x1, waiting for transfers between devices, shards(): lax.psum_scatter(grad_wup.astype(jnp.bfloat16), 'shard', scatter_dimensio...  61.1 us
    reduce_scatter x1, waiting for transfers between devices, shards(): lax.psum_scatter(grad_wdown.astype(jnp.bfloat16), 'shard', scatter_dimens...  60.8 us
    reduce_scatter x1, waiting for transfers between devices, shards(): lax.psum_scatter(grad_wgate.astype(jnp.bfloat16), 'shard', scatter_dimens...  58.1 us
    another operation x4, other arithmetic  41.7 us
  transfers between devices with their start and end apart: 15, of which 8 were waited for; matrix products, arithmetic and copies ran while one was open for 39% of the time, Pallas kernels for 0%

commit v1 on v0

v1 whole, which is shorter than its diff:
```python
import jax
import jax.numpy as jnp
from jax import lax
from jax.experimental import pallas as pl
from jax.experimental.pallas import tpu as pltpu
from jax.sharding import PartitionSpec as P

H = 16
KV = 8
HD = 128
SEQ_LEN = 1024
LONGEST = 512
ROWS = 256
WINDOW = LONGEST + ROWS
PARTS = 1
PAIR = H // KV * HD
VMEM_LIMIT = 56 * 1024 * 1024


norm_epsilon = 1e-06
rotary_base = 1000000.0


def doc_layout(lengths, seq_length):
    bounds = jnp.cumsum(lengths, axis=-1)
    places = lax.broadcasted_iota(jnp.int32, (seq_length,), 0)
    passed = (places[None, :, None] >= bounds[:, None, :]).astype(jnp.int32)
    segment = jnp.sum(passed, axis=-1)
    begins = jnp.sum(passed * lengths[:, None, :], axis=-1)
    return (segment, places[None, :] - begins)


def rotary_tables(position, head_size):
    halves = jnp.arange(head_size // 2, dtype=jnp.float32)
    frequency = rotary_base ** (-(2.0 / head_size) * halves)
    angles = position.astype(jnp.float32)[..., None] * frequency
    cosine = jnp.cos(angles)
    sine = jnp.sin(angles)
    return (jnp.concatenate([cosine, cosine], -1), jnp.concatenate([sine, sine], -1))


def norm_forward(value, gain):
    factor = lax.rsqrt(jnp.mean(value * value, axis=-1, keepdims=True) + norm_epsilon)
    return (value * factor * gain, factor)


def norm_backward(value, factor, gain, gradient):
    scaled = gradient * gain
    inner = jnp.mean(scaled * value, axis=-1, keepdims=True)
    return (factor * (scaled - value * factor * factor * inner), gradient * value * factor)


def dot(left, right):
    return jnp.dot(left, right, preferred_element_type=jnp.float32)


def across_rows(left, right):
    return lax.dot_general(
        left, right, (((0,), (0,)), ((), ())), preferred_element_type=jnp.float32
    )


def against_rows(left, right):
    return lax.dot_general(
        left, right, (((1,), (1,)), ((), ())), preferred_element_type=jnp.float32
    )


def windows():
    for start in range(0, SEQ_LEN, ROWS):
        yield start, max(0, start - LONGEST), start + ROWS


def turn(value, cosine, sine):
    return value * cosine + pltpu.roll(value, HD // 2, 1) * sine


def turn_back(value, cosine, sine):
    return value * cosine - pltpu.roll(value, HD // 2, 1) * sine


def fill_mask(mask_ref, segment_column, segment_row):
    for start, first, end in windows():
        rows = start + lax.broadcasted_iota(jnp.int32, (ROWS, end - first), 0)
        columns = first + lax.broadcasted_iota(jnp.int32, (ROWS, end - first), 1)
        same = segment_column[start:end, :] == segment_row[:, first:end]
        mask_ref[start:end, 0 : end - first] = jnp.where(
            same & (columns <= rows), 1.0, 0.0
        )


def attention_forward_kernel(
    acts, w_query, w_key, w_value, gain_query, gain_key, cosine, sine, seg_col, seg_row,
    query_normed, key_normed, values, attended, stats, mask,
):
    @pl.when(pl.program_id(0) == 0)
    def _():
        fill_mask(mask, seg_col, seg_row)

    cos, sin = cosine[...], sine[...]
    key = dot(acts[...], w_key[...])
    key_factor = lax.rsqrt(jnp.mean(key * key, axis=-1, keepdims=True) + norm_epsilon)
    key = key * key_factor
    key_normed[...] = key.astype(jnp.bfloat16)
    key = turn(key * gain_key[...], cos, sin).astype(jnp.bfloat16)
    value = dot(acts[...], w_value[...]).astype(jnp.bfloat16)
    values[...] = value
    stats[0, :, 4:5] = key_factor
    raw = dot(acts[...], w_query[...])
    for head in range(H // KV):
        lanes = slice(head * HD, (head + 1) * HD)
        query = raw[:, lanes]
        factor = lax.rsqrt(jnp.mean(query * query, axis=-1, keepdims=True) + norm_epsilon)
        query = query * factor
        query_normed[:, lanes] = query.astype(jnp.bfloat16)
        query = turn(query * gain_query[...], cos, sin).astype(jnp.bfloat16)
        stats[0, :, head : head + 1] = factor
        for start, first, end in windows():
            scores = against_rows(query[start:end], key[first:end])
            weights = jnp.exp(scores) * mask[start:end, 0 : end - first]
            total = jnp.sum(weights, axis=-1, keepdims=True)
            summed = dot(weights.astype(jnp.bfloat16), value[first:end])
            attended[start:end, lanes] = (summed / total).astype(jnp.bfloat16)
            stats[0, start:end, 2 + head : 3 + head] = jnp.log(total)


def attention_backward_kernel(
    acts_turned, grad_attn, w_query, w_key, w_value, w_output, gain_query, gain_key,
    cosine, sine, seg_col, seg_row, query_normed, key_normed, values, attended, stats, before,
    grad_wquery, grad_wkey, grad_wvalue, grad_acts, grad_gain_query, grad_gain_key,
    mask, grad_key, grad_value, grad_query, turned_back,
):
    scale = HD ** (-0.5)

    @pl.when(pl.program_id(0) == 0)
    def _():
        fill_mask(mask, seg_col, seg_row)
        grad_acts[...] = before[...]
        grad_gain_query[...] = jnp.zeros_like(grad_gain_query)
        grad_gain_key[...] = jnp.zeros_like(grad_gain_key)

    cos, sin = cosine[...], sine[...]
    grad_out = against_rows(grad_attn[...], w_output[...]).astype(jnp.bfloat16)
    normed = key_normed[...].astype(jnp.float32)
    key = turn(normed * gain_key[...], cos, sin).astype(jnp.bfloat16)
    value = values[...]
    grad_key[...] = jnp.zeros_like(grad_key)
    grad_value[...] = jnp.zeros_like(grad_value)
    for head in range(H // KV):
        lanes = slice(head * HD, (head + 1) * HD)
        normed = query_normed[:, lanes].astype(jnp.float32)
        query = turn(normed * (gain_query[...] * scale), cos, sin).astype(jnp.bfloat16)
        grad_head = grad_out[:, lanes]
        delta = jnp.sum(
            grad_head.astype(jnp.float32) * attended[:, lanes].astype(jnp.float32),
            axis=-1,
            keepdims=True,
        )
        for start, first, end in windows():
            scores = against_rows(query[start:end], key[first:end])
            probs = (
                jnp.exp(scores - stats[0, start:end, 2 + head : 3 + head])
                * mask[start:end, 0 : end - first]
            )
            grad_probs = against_rows(grad_head[start:end], value[first:end])
            grad_scores = (probs * (grad_probs - delta[start:end])).astype(jnp.bfloat16)
            turned_back[start:end, :] = dot(grad_scores, key[first:end]) * scale
            grad_key[first:end, :] += across_rows(grad_scores, query[start:end])
            grad_value[first:end, :] += across_rows(
                probs.astype(jnp.bfloat16), grad_head[start:end]
            )
        turned = turn_back(turned_back[...], cos, sin)
        grad_gain_query[...] += jnp.sum(turned * normed, axis=0, keepdims=True)
        turned = turned * gain_query[...]
        inner = jnp.mean(turned * normed, axis=-1, keepdims=True)
        grad_query[:, lanes] = (
            stats[0, :, head : head + 1] * (turned - normed * inner)
        ).astype(jnp.bfloat16)
    normed = key_normed[...].astype(jnp.float32)
    turned = turn_back(grad_key[...], cos, sin)
    grad_gain_key[...] += jnp.sum(turned * normed, axis=0, keepdims=True)
    turned = turned * gain_key[...]
    inner = jnp.mean(turned * normed, axis=-1, keepdims=True)
    low_key = (stats[0, :, 4:5] * (turned - normed * inner)).astype(jnp.bfloat16)
    low_value = grad_value[...].astype(jnp.bfloat16)
    low_query = grad_query[...]
    grad_wquery[...] = dot(acts_turned[...], low_query).astype(jnp.bfloat16)
    grad_wkey[...] = dot(acts_turned[...], low_key).astype(jnp.bfloat16)
    grad_wvalue[...] = dot(acts_turned[...], low_value).astype(jnp.bfloat16)
    grad_acts[...] += (
        against_rows(low_query, w_query[...])
        + against_rows(low_key, w_key[...])
        + against_rows(low_value, w_value[...])
    )


def feedforward_kernel(
    acts, acts_turned, branch, w_gate, w_up, w_down,
    summed, grad_acts, grad_wgate, grad_wup, grad_wdown,
):
    @pl.when(pl.program_id(0) == 0)
    def _():
        summed[...] = jnp.zeros_like(summed)
        grad_acts[...] = jnp.zeros_like(grad_acts)

    gate = dot(acts[...], w_gate[...])
    up = dot(acts[...], w_up[...])
    sigmoid = jax.nn.sigmoid(gate)
    swish = gate * sigmoid
    hidden = (swish * up).astype(jnp.bfloat16)
    summed[...] += dot(hidden, w_down[...])
    grad_hidden = against_rows(branch[...], w_down[...])
    grad_up = (grad_hidden * swish).astype(jnp.bfloat16)
    grad_gate = (grad_hidden * up * (sigmoid + swish * (1.0 - sigmoid))).astype(jnp.bfloat16)
    grad_wdown[...] = across_rows(hidden, branch[...]).astype(jnp.bfloat16)
    grad_wgate[...] = dot(acts_turned[...], grad_gate).astype(jnp.bfloat16)
    grad_wup[...] = dot(acts_turned[...], grad_up).astype(jnp.bfloat16)
    grad_acts[...] += against_rows(grad_gate, w_gate[...]) + against_rows(grad_up, w_up[...])


def whole(shape):
    return pl.BlockSpec(shape, lambda step: (0,) * len(shape))


def columns(rows, width, first=0):
    return pl.BlockSpec((rows, width), lambda step: (0, step + first))


def sds(shape, dtype=jnp.bfloat16):
    return jax.ShapeDtypeStruct(shape, dtype)


def params():
    return pltpu.CompilerParams(
        dimension_semantics=("arbitrary",), vmem_limit_bytes=VMEM_LIMIT
    )


def attention_forward(acts, w_query, w_key, w_value, tables):
    rows, width = acts.shape
    return pl.pallas_call(
        attention_forward_kernel,
        grid=(KV,),
        in_specs=[
            whole((rows, width)), columns(width, PAIR), columns(width, HD), columns(width, HD),
            whole((1, HD)), whole((1, HD)), whole((rows, HD)), whole((rows, HD)),
            whole((rows, 1)), whole((1, rows)),
        ],
        out_specs=[
            columns(rows, PAIR), columns(rows, HD), columns(rows, HD), columns(rows, PAIR),
            pl.BlockSpec((1, rows, 8), lambda step: (step, 0, 0)),
        ],
        out_shape=[
            sds((rows, H * HD)), sds((rows, KV * HD)), sds((rows, KV * HD)),
            sds((rows, H * HD)), sds((KV, rows, 8), jnp.float32),
        ],
        scratch_shapes=[pltpu.VMEM((rows, WINDOW), jnp.float32)],
        compiler_params=params(),
        cost_estimate=pl.CostEstimate(
            flops=2 * rows * width * 4096 + 6 * 10**9,
            bytes_accessed=26 * 2**20,
            transcendentals=10**7,
        ),
        name="attention_forward",
    )(acts, w_query, w_key, w_value, *tables)


def attention_backward(acts_turned, grad_attn, weights, tables, kept, before, first, count):
    w_query, w_key, w_value, w_output = weights
    rows, width = grad_attn.shape
    return pl.pallas_call(
        attention_backward_kernel,
        grid=(count,),
        in_specs=[
            whole((width, rows)), whole((rows, width)),
            columns(width, PAIR, first), columns(width, HD, first), columns(width, HD, first),
            pl.BlockSpec((PAIR, width), lambda step: (step + first, 0)),
            whole((1, HD)), whole((1, HD)), whole((rows, HD)), whole((rows, HD)),
            whole((rows, 1)), whole((1, rows)),
            columns(rows, PAIR, first), columns(rows, HD, first), columns(rows, HD, first),
            columns(rows, PAIR, first),
            pl.BlockSpec((1, rows, 8), lambda step: (step + first, 0, 0)),
            whole((rows, width)),
        ],
        out_specs=[
            columns(width, PAIR), columns(width, HD), columns(width, HD),
            whole((rows, width)), whole((1, HD)), whole((1, HD)),
        ],
        out_shape=[
            sds((width, count * PAIR)), sds((width, count * HD)), sds((width, count * HD)),
            sds((rows, width), jnp.float32), sds((1, HD), jnp.float32),
            sds((1, HD), jnp.float32),
        ],
        scratch_shapes=[
            pltpu.VMEM((rows, WINDOW), jnp.float32),
            pltpu.VMEM((rows, HD), jnp.float32),
            pltpu.VMEM((rows, HD), jnp.float32),
            pltpu.VMEM((rows, PAIR), jnp.bfloat16),
            pltpu.VMEM((rows, HD), jnp.float32),
        ],
        compiler_params=params(),
        cost_estimate=pl.CostEstimate(
            flops=(2 * rows * width * 1280 + 2 * 10**9) * count,
            bytes_accessed=(5 * count + 12) * 2**20,
            transcendentals=count * 10**6,
        ),
        name="attention_backward",
    )(acts_turned, grad_attn, w_query, w_key, w_value, w_output, *tables, *kept, before)


def feedforward(acts, acts_turned, branch, w_gate, w_up, w_down):
    rows, width = acts.shape
    units = w_gate.shape[1]
    down_spec = pl.BlockSpec((ROWS, width), lambda step: (step, 0))
    return pl.pallas_call(
        feedforward_kernel,
        grid=(units // ROWS,),
        in_specs=[
            whole((rows, width)), whole((width, rows)), whole((rows, width)),
            columns(width, ROWS), columns(width, ROWS), down_spec,
        ],
        out_specs=[
            whole((rows, width)), whole((rows, width)),
            columns(width, ROWS), columns(width, ROWS), down_spec,
        ],
        out_shape=[
            sds((rows, width), jnp.float32), sds((rows, width), jnp.float32),
            sds((width, units)), sds((width, units)), sds((units, width)),
        ],
        compiler_params=params(),
        cost_estimate=pl.CostEstimate(
            flops=18 * rows * width * units, bytes_accessed=52 * 2**20,
            transcendentals=rows * units,
        ),
        name="feedforward",
    )(acts, acts_turned, branch, w_gate, w_up, w_down)


def add_up(parts):
    total = parts[0].astype(jnp.float32)
    for part in parts[1:]:
        total = total + part.astype(jnp.float32)
    return total


def swap(value, axis, bit):
    size = lax.axis_size(axis)
    return lax.ppermute(value, axis, [(i, i ^ (1 << bit)) for i in range(size)])


def bits_of(axis):
    return lax.axis_size(axis).bit_length() - 1


def my_bit(axis, bit):
    return (lax.axis_index(axis) >> bit) & 1


def halve(value, axis, order):
    count = bits_of(axis)
    rows, width = value.shape
    value = value.reshape((2,) * count + (rows >> count, width))
    left = list(range(count))[::-1]
    for bit in order:
        place = left.index(bit)
        left.remove(bit)
        mine = my_bit(axis, bit)
        theirs = swap(lax.dynamic_index_in_dim(value, 1 - mine, place, False), axis, bit)
        own = lax.dynamic_index_in_dim(value, mine, place, False)
        value = (own.astype(jnp.float32) + theirs.astype(jnp.float32)).astype(value.dtype)
    return value


def double(value, axis, order):
    left = []
    for bit in order[::-1]:
        place = sum(1 for other in left if other > bit)
        left.append(bit)
        theirs = swap(value, axis, bit)
        mine = my_bit(axis, bit) == 0
        value = jnp.stack(
            [jnp.where(mine, value, theirs), jnp.where(mine, theirs, value)], place
        )
    return value.reshape((-1, value.shape[-1]))


def reduce_rows(parts, late):
    owned = halve(
        add_up(parts).astype(jnp.bfloat16), "shard", list(range(bits_of("shard")))
    )
    order = list(range(bits_of("replica")))
    order = order[1:] + order[:1] if late else order
    return double(halve(owned, "replica", order), "replica", order)


def sum_everywhere(value):
    for axis in ("shard", "replica"):
        for bit in range(bits_of(axis)):
            value = value + swap(value, axis, bit)
    return value


def shards(
    tokens, lengths, attention_gain, query_weight, key_weight, value_weight, query_gain,
    key_gain, output_weight, feedforward_gain, gate_weight, up_weight, down_weight, cotangent,
):
    def gather(array):
        return lax.all_gather(array, "shard", axis=0, tiled=True)

    gains = lax.all_gather(
        jnp.concatenate([attention_gain, feedforward_gain, query_gain, key_gain]), "shard", axis=0
    ).astype(jnp.float32)
    slim, narrow = attention_gain.shape[0], query_gain.shape[0]
    gain_one = gains[:, :slim].reshape(-1)
    gain_two = gains[:, slim : 2 * slim].reshape(-1)
    gain_query = gains[:, 2 * slim : 2 * slim + narrow].reshape(1, -1)
    gain_key = gains[:, 2 * slim + narrow :].reshape(1, -1)
    w_key, w_value, w_query = gather(key_weight), gather(value_weight), gather(query_weight)
    w_output = gather(output_weight)
    w_gate, w_up, w_down = gather(gate_weight), gather(up_weight), gather(down_weight)
    segment, position = doc_layout(lengths, SEQ_LEN)
    cosine, sine = rotary_tables(position, HD)
    half = HD // 2
    sine = jnp.concatenate([-sine[..., :half], sine[..., half:]], -1)
    scale = HD ** (-0.5)
    local_seqs = lengths.shape[0]
    x = tokens.astype(jnp.float32).reshape(local_seqs, SEQ_LEN, -1)
    dy = cotangent.reshape(local_seqs, SEQ_LEN, -1)
    seqs = range(local_seqs)
    mixed, states = [], []
    grads_gate, grads_up, grads_down, gain_two_terms = [], [], [], []
    for s in seqs:
        normed, factor_one = norm_forward(x[s], gain_one)
        acts = normed.astype(jnp.bfloat16)
        tables = (cosine[s], sine[s], segment[s][:, None], segment[s][None, :])
        query_normed, key_normed, values, attended, stats = attention_forward(
            acts, w_query, w_key, w_value, (gain_query * scale, gain_key, *tables)
        )
        middle = x[s] + dot(attended, w_output)
        normed_two, factor_two = norm_forward(middle, gain_two)
        acts_two = normed_two.astype(jnp.bfloat16)
        summed, grad_acts_two, grad_wgate, grad_wup, grad_wdown = feedforward(
            acts_two, acts_two.T, dy[s], w_gate, w_up, w_down
        )
        mixed.append((middle + summed).astype(jnp.bfloat16))
        grads_gate.append(grad_wgate)
        grads_up.append(grad_wup)
        grads_down.append(grad_wdown)
        grad_norm_two, terms = norm_backward(middle, factor_two, gain_two, grad_acts_two)
        gain_two_terms.append(jnp.sum(terms, axis=0))
        grad_middle = dy[s].astype(jnp.float32) + grad_norm_two
        kept = (query_normed, key_normed, values, attended, stats)
        states.append((acts, factor_one, tables, kept, grad_middle))
    out_gate, out_up = reduce_rows(grads_gate, False), reduce_rows(grads_up, True)
    out_down = reduce_rows(grads_down, True)
    low = [state[4].astype(jnp.bfloat16) for state in states]
    out_output = reduce_rows([across_rows(states[s][3][3], low[s]) for s in seqs], False)
    weights = (w_query, w_key, w_value, w_output)
    turned = [state[0].T for state in states]
    grad_acts = [jnp.zeros((SEQ_LEN, tokens.shape[1]), jnp.float32) for s in seqs]
    gain_query_terms, gain_key_terms = [], []
    outs = []
    count = KV // PARTS
    for part in range(PARTS):
        grads = []
        for s in seqs:
            tables = (gain_query, gain_key, *states[s][2])
            *weight_grads, grad_acts[s], query_term, key_term = attention_backward(
                turned[s], low[s], weights, tables, states[s][3], grad_acts[s], part * count, count
            )
            grads.append(weight_grads)
            gain_query_terms.append(query_term[0])
            gain_key_terms.append(key_term[0])
        outs.append([add_up(parts).astype(jnp.bfloat16) for parts in zip(*grads)])
    grads = [jnp.concatenate(parts, axis=1) for parts in zip(*outs)]
    out_query = reduce_rows(grads[:1], False).astype(jnp.float32)
    both = reduce_rows([jnp.concatenate(grads[1:], axis=1)], True).astype(jnp.float32)
    out_key, out_value = both[:, : KV * HD], both[:, KV * HD :]
    grad_tokens, gain_one_terms = [], []
    for s in seqs:
        grad_norm_one, terms = norm_backward(x[s], states[s][1], gain_one, grad_acts[s])
        gain_one_terms.append(jnp.sum(terms, axis=0))
        grad_tokens.append(states[s][4] + grad_norm_one)
    small = sum_everywhere(
        jnp.concatenate(
            [add_up(t) for t in (gain_one_terms, gain_two_terms, gain_query_terms, gain_key_terms)]
        ).reshape(-1, HD)
    ).reshape(-1)
    place = lax.axis_index("shard")
    model = slim * lax.axis_size("shard")

    def own(start, size):
        return lax.dynamic_slice(small, (start + place * size,), (size,))

    return (
        jnp.concatenate(mixed),
        jnp.concatenate(grad_tokens),
        own(0, slim),
        out_query,
        out_key,
        out_value,
        own(2 * model, narrow),
        own(2 * model + HD, narrow),
        out_output.astype(jnp.float32),
        own(model, slim),
        out_gate.astype(jnp.float32),
        out_up.astype(jnp.float32),
        out_down.astype(jnp.float32),
    )


def solution(mesh):
    return jax.shard_map(
        shards,
        mesh=mesh,
        in_specs=(
            P(("replica", "shard"), None),
            P(("replica", "shard"), None),
            P("shard"),
            P("shard", None),
            P("shard", None),
            P("shard", None),
            P("shard"),
            P("shard"),
            P("shard", None),
            P("shard"),
            P("shard", None),
            P("shard", None),
            P("shard", None),
            P(("replica", "shard"), None),
        ),
        out_specs=(
            P(("replica", "shard"), None),
            P(("replica", "shard"), None),
            P("shard"),
            P("shard", None),
            P("shard", None),
            P("shard", None),
            P("shard"),
            P("shard"),
            P("shard", None),
            P("shard"),
            P("shard", None),
            P("shard", None),
            P("shard", None),
        ),
        check_vma=False,
    )
```

time: 1230 us -> 836 us (0.68)
  matrix products: 343 us -> 13.3 us
  Pallas kernels: 0 us -> 210 us
  other arithmetic: 214 us -> 65.6 us
  local copies, waits for them, and re-layouts: 130 us -> 39.9 us
  blocking collectives: 59.1 us -> 8.5 us
  starting transfers between devices: 0.6 us -> 47.4 us
  waiting for transfers between devices: 464 us -> 426 us
    reduce_scatter x7 -> x0, waiting for transfers between devices: 272 us -> none  [the longest x1 71.8 us: shards(): lax.psum_scatter(grad_woutput, 'shard', scatter_dimension=0, tiled=True)]
    dot_general x26 -> x1, matrix products: 275 us -> 8.44 us  [dot(): return jnp.dot(left, right, preferred_element_type=jnp.float32)]
    ppermute x0 -> x53, waiting for transfers between devices: none -> 246 us  [swap(): return lax.ppermute(value, axis, [(i, i ^ 1 << bit) for i in range(size)])]
    pallas_call x0 -> x3, Pallas kernels: none -> 210 us  [the longest x1 97.4 us: attention_backward(): pl.pallas_call(attention_backward_kernel, grid=(count,), in_specs=[whole(...]
    psum x1 -> x0, waiting for transfers between devices: 186 us -> none  [shards(): lax.psum(attn_owned[1].astype(jnp.bfloat16), 'replica').astype(jnp.float32)]
    all_gather x7, waiting for transfers between devices: 1.34 us -> 175 us  [gather(): return lax.all_gather(array, 'shard', axis=0, tiled=True)]
    dot_general x7 -> x1, matrix products: 68.6 us -> 4.9 us  [across_rows(): lax.dot_general(left, right, (((0,), (0,)), ((), ())), preferred_element_...]
    ppermute x0 -> x53, starting transfers between devices: none -> 47.1 us  [swap(): return lax.ppermute(value, axis, [(i, i ^ 1 << bit) for i in range(size)])]
  transfers between devices with their start and end apart: 15 -> 60, of which waited for: 8 -> 34; matrix products, arithmetic and copies ran while one was open for 39% -> 13% of each run, Pallas kernels for 0% -> 17%
where the time goes in v1:
time: 836 us; the launch traced here: 827 us
  waiting for transfers between devices  426 us (51%)
  Pallas kernels  210 us (25%)
  other arithmetic  65.6 us (8%)
  starting transfers between devices  47.4 us (6%)
  local copies, waits for them, and re-layouts  39.9 us (5%)
  between operations  16.4 us (2%)
  matrix products  13.3 us (2%)
  blocking collectives  8.5 us (1%)
    ppermute x53, waiting for transfers between devices, swap(): return lax.ppermute(value, axis, [(i, i ^ 1 << bit) for i in range(size)])  246 us
    all_gather x7, waiting for transfers between devices, gather(): return lax.all_gather(array, 'shard', axis=0, tiled=True)  175 us
    pallas_call x1, Pallas kernels, attention_backward(): pl.pallas_call(attention_backward_kernel, grid=(count,), in_specs=[whole(...  97.4 us
    pallas_call x1, Pallas kernels, feedforward(): pl.pallas_call(feedforward_kernel, grid=(units // ROWS,), in_specs=[whole...  69.2 us
    ppermute x53, starting transfers between devices, swap(): return lax.ppermute(value, axis, [(i, i ^ 1 << bit) for i in range(size)])  47.1 us
    pallas_call x1, Pallas kernels, attention_forward(): pl.pallas_call(attention_forward_kernel, grid=(KV,), in_specs=[whole((row...  43.1 us
    convert_element_type x30, other arithmetic, halve(): (own.astype(jnp.float32) + theirs.astype(jnp.float32)).astype(value.dtype)  25.8 us
    squeeze x27, local copies, waits for them, and re-layouts, halve(): lax.dynamic_index_in_dim(value, 1 - mine, place, False)  18.6 us
  transfers between devices with their start and end apart: 60, of which 34 were waited for; matrix products, arithmetic and copies ran while one was open for 13% of the time, Pallas kernels for 17%

profile of v1, /device:TPU:0, one launch (start us, length us, event | category | flops | bytes accessed | tf_op | source)
XLA Modules:
  0.0 826.5 jit_solution(7239936769987068062)
XLA Ops:
  13.7 8.5 %all-reduce = bf16[2304]{0:T(1024)(128)(2,1)S(1)} all-reduce(bf16[2304]{0:T(1024)(128)(2,1)S(1)} %dynamic-update-slice), channel_id=2, replica_groups=mesh['replica'=8,'shard'=4] {'shard'}, use_global_device_ids=true, to_apply=%add | all-reduce | flops 2304 | bytes 9216
  36.2 23.0 %all-gather.13.cloned.1.call-done.w_value = bf16[1024,1024]{1,0:T(8,128)(2,1)} async-done(((bf16[256,1024]{1,0:T(8,128)(2,1)}), bf16[1024,1024]{1,0:T(8,128)(2,1)}) %all-gather.13.cloned.1.call-update) | async-done | bytes 2097168 | tf_op jit(solution)/shard_map/all_gather | solution.py:408
  59.2 36.1 %all-gather.9.cloned.1.call-done.w_query = bf16[1024,2048]{1,0:T(8,128)(2,1)} async-done(((bf16[256,2048]{1,0:T(8,128)(2,1)}), bf16[1024,2048]{1,0:T(8,128)(2,1)}) %all-gather.9.cloned.1.call-update) | async-done | bytes 4194320 | tf_op jit(solution)/shard_map/all_gather | solution.py:408
  95.2 43.1 %attention_forward.1 = (bf16[1024,2048]{1,0:T(8,128)(2,1)}, bf16[1024,1024]{1,0:T(8,128)(2,1)}, bf16[1024,1024]{1,0:T(8,128)(2,1)}, bf16[1024,2048]{1,0:T(8,128)(2,1)}, f32[8,1024,8]{2,1,0:T(8,128)}) custom-call(bf16[1024,1024]{1,0:T(8,128)(2,1)} %fusion.5.acts, bf16[1024,2048]{1,0:T(8,128)(2,1)} %all-gather.9.cloned.1.call-done.w_query, ...), custom_call_target="tpu_custom_call" | custom-call | flops 14589934592 | bytes 27262976 | tf_op jit(solution)/shard_map/attention_forward/pallas_call | solution.py:241
  138.3 8.4 %multiply_reduce_fusion.2 = (f32[1024]{0:T(1024)S(1)}, f32[1024,1024]{1,0:T(8,128)S(1)}) fusion(bf16[1024,2048]{1,0:T(8,128)(2,1)} %get-tuple-element.29.attended, bf16[2048,1024]{1,0:T(8,128)(2,1)} %all-gather.15.cloned.1.call-done.w_output, bf16[1024,1024]{1,0:T(8,128)(2,1)S(1)} %copy-done.2), kind=kOutput, calls=%fused_computation.34 | convolution fusion | flops 4299160576 | bytes 14684160 | tf_op jit(solution)/shard_map/dot_general | solution.py:54
  158.4 20.6 %all-gather.17.cloned.1.call-done.w_gate = bf16[1024,3072]{1,0:T(8,128)(2,1)} async-done(((bf16[256,3072]{1,0:T(8,128)(2,1)}), bf16[1024,3072]{1,0:T(8,128)(2,1)}) %all-gather.17.cloned.1.call-update) | async-done | bytes 6291472 | tf_op jit(solution)/shard_map/all_gather | solution.py:408
  179.0 47.8 %all-gather.19.cloned.1.call-done.w_up = bf16[1024,3072]{1,0:T(8,128)(2,1)} async-done(((bf16[256,3072]{1,0:T(8,128)(2,1)}), bf16[1024,3072]{1,0:T(8,128)(2,1)}) %all-gather.19.cloned.1.call-update) | async-done | bytes 6291472 | tf_op jit(solution)/shard_map/all_gather | solution.py:408
  226.8 48.0 %all-gather.21.cloned.1.call-done.w_down = bf16[3072,1024]{1,0:T(8,128)(2,1)} async-done(((bf16[768,1024]{1,0:T(8,128)(2,1)}), bf16[3072,1024]{1,0:T(8,128)(2,1)}) %all-gather.21.cloned.1.call-update) | async-done | bytes 6291472 | tf_op jit(solution)/shard_map/all_gather | solution.py:408
  274.8 69.2 %feedforward.1 = (f32[1024,1024]{1,0:T(8,128)}, f32[1024,1024]{1,0:T(8,128)}, bf16[1024,3072]{1,0:T(8,128)(2,1)}, bf16[1024,3072]{1,0:T(8,128)(2,1)}, bf16[3072,1024]{1,0:T(8,128)(2,1)}) custom-call(bf16[1024,1024]{1,0:T(8,128)(2,1)} %multiply_convert_fusion.acts, bf16[1024,1024]{1,0:T(8,128)(2,1)} %copy.73.acts_turned, bf16[1024,1024]{1,0:T(8,128)(2,1)} %branch.1, ...), custom_call_target="tpu_custom_call" | custom-call | flops 57982058496 | bytes 54525952 | tf_op jit(solution)/shard_map/feedforward/pallas_call | solution.py:315
  356.2 4.9 convolution_convert_fusion
  367.4 97.4 %attention_backward.1 = (bf16[1024,2048]{1,0:T(8,128)(2,1)}, bf16[1024,1024]{1,0:T(8,128)(2,1)}, bf16[1024,1024]{1,0:T(8,128)(2,1)}, f32[1024,1024]{1,0:T(8,128)}, f32[1,128]{1,0:T(1,128)}, /*index=5*/f32[1,128]{1,0:T(1,128)}) custom-call(bf16[1024,1024]{1,0:T(8,128)(2,1)} %copy.74.acts_turned, bf16[1024,1024]{1,0:T(8,128)(2,1)} %copy-done.12, ...), custom_call_target="tpu_custom_call" | custom-call | flops 37474836480 | bytes 54525952 | tf_op jit(solution)/shard_map/attention_backward/pallas_call | solution.py:271
  478.7 6.4 fusion.9
  519.1 4.8 collective-permute-done.22
  526.1 20.3 %collective-permute-done.14 = bf16[256,2048]{1,0:T(8,128)(2,1)} collective-permute-done((bf16[256,2048]{1,0:T(8,128)(2,1)}, bf16[256,2048]{1,0:T(8,128)(2,1)}, u32[]{:S(2)}, u32[]{:S(2)}) %collective-permute-start.14) | collective-permute-done | bytes 1048608 | tf_op jit(solution)/shard_map/ppermute | solution.py:348
  549.5 19.3 %collective-permute-done.6 = bf16[256,2048]{1,0:T(8,128)(2,1)} collective-permute-done((bf16[256,2048]{1,0:T(8,128)(2,1)}, bf16[256,2048]{1,0:T(8,128)(2,1)}, u32[]{:S(2)}, u32[]{:S(2)}) %collective-permute-start.6) | collective-permute-done | bytes 1048608 | tf_op jit(solution)/shard_map/ppermute | solution.py:348
  572.8 8.0 collective-permute-done.15
  585.4 8.2 collective-permute-done.24
  597.0 4.4 collective-permute-done.8
  610.4 7.4 collective-permute-done.26
  620.7 6.0 collective-permute-done.10
  631.2 5.6 collective-permute-done.19
  637.7 4.8 collective-permute-done.11
  648.1 20.8 %collective-permute-done.30 = bf16[256,3072]{1,0:T(8,128)(2,1)S(1)} collective-permute-done((bf16[256,3072]{1,0:T(8,128)(2,1)S(1)}, bf16[256,3072]{1,0:T(8,128)(2,1)S(1)}, u32[]{:S(2)}, u32[]{:S(2)}) %collective-permute-start.30) | collective-permute-done | bytes 1572896 | tf_op jit(solution)/shard_map/ppermute | solution.py:348
  680.1 15.8 %collective-permute-done.39 = bf16[2,2,32,3072]{3,2,1,0:T(8,128)(2,1)S(1)} collective-permute-done((bf16[2,2,32,3072]{3,2,1,0:T(8,128)(2,1)S(1)}, bf16[2,2,32,3072]{3,2,1,0:T(8,128)(2,1)S(1)}, u32[]{:S(2)}, u32[]{:S(2)}) %collective-permute-start.39) | collective-permute-done | bytes 786464 | tf_op jit(solution)/shard_map/ppermute | solution.py:348
  700.2 14.2 %collective-permute-done.40 = bf16[2,32,3072]{2,1,0:T(8,128)(2,1)S(1)} collective-permute-done((bf16[2,32,3072]{2,1,0:T(8,128)(2,1)S(1)}, bf16[2,32,3072]{2,1,0:T(8,128)(2,1)S(1)}, u32[]{:S(2)}, u32[]{:S(2)}) %collective-permute-start.40) | collective-permute-done | bytes 393248 | tf_op jit(solution)/shard_map/ppermute | solution.py:348
  717.1 5.4 collective-permute-done.41
  730.3 25.3 %collective-permute-done.34 = bf16[32,3072]{1,0:T(8,128)(2,1)S(1)} collective-permute-done((bf16[32,3072]{1,0:T(8,128)(2,1)S(1)}, bf16[32,3072]{1,0:T(8,128)(2,1)S(1)}, u32[]{:S(2)}, u32[]{:S(2)}) %collective-permute-start.34) | collective-permute-done | bytes 196640 | tf_op jit(solution)/shard_map/ppermute | solution.py:348
  755.7 8.4 %collective-permute-done.51 = bf16[2,96,1024]{2,1,0:T(8,128)(2,1)S(1)} collective-permute-done((bf16[2,96,1024]{2,1,0:T(8,128)(2,1)S(1)}, bf16[2,96,1024]{2,1,0:T(8,128)(2,1)S(1)}, u32[]{:S(2)}, u32[]{:S(2)}) %collective-permute-start.51) | collective-permute-done | bytes 393248 | tf_op jit(solution)/shard_map/ppermute | solution.py:348
  764.3 8.1 collective-permute-done.43
  772.7 8.2 collective-permute-done.35
  781.6 16.1 %collective-permute-done.52 = bf16[2,2,96,1024]{3,2,1,0:T(8,128)(2,1)S(1)} collective-permute-done((bf16[2,2,96,1024]{3,2,1,0:T(8,128)(2,1)S(1)}, bf16[2,2,96,1024]{3,2,1,0:T(8,128)(2,1)S(1)}, u32[]{:S(2)}, u32[]{:S(2)}) %collective-permute-start.52) | collective-permute-done | bytes 786464 | tf_op jit(solution)/shard_map/ppermute | solution.py:348
  800.1 14.3 %collective-permute-done.44 = bf16[2,2,32,3072]{3,2,1,0:T(8,128)(2,1)S(1)} collective-permute-done((bf16[2,2,32,3072]{3,2,1,0:T(8,128)(2,1)S(1)}, bf16[2,2,32,3072]{3,2,1,0:T(8,128)(2,1)S(1)}, u32[]{:S(2)}, u32[]{:S(2)}) %collective-permute-start.44) | collective-permute-done | bytes 786464 | tf_op jit(solution)/shard_map/ppermute | solution.py:348
  (318 shorter events, 171.3 us)
Async XLA Ops:
  7.2 29.0 %all-gather.11.cloned.1.call-start = ((), (), s32[]{:S(2)}) async-start(), calls=%async_computation.1 | async-start | bytes 2621440 | tf_op jit(solution)/shard_map/all_gather | solution.py:408
  7.9 51.2 %all-gather.13.cloned.1.call-start = ((), (), s32[]{:S(2)}) async-start(), calls=%async_computation.2 | async-start | bytes 2621440 | tf_op jit(solution)/shard_map/all_gather | solution.py:408
  8.7 86.6 %all-gather.9.cloned.1.call-start = ((), (), s32[]{:S(2)}) async-start(), calls=%async_computation | async-start | bytes 5242880 | tf_op jit(solution)/shard_map/all_gather | solution.py:408
  9.5 128.9 %all-gather.15.cloned.1.call-start = ((), (), s32[]{:S(2)}) async-start(), calls=%async_computation.3 | async-start | bytes 5242880 | tf_op jit(solution)/shard_map/all_gather | solution.py:408
  10.0 169.0 %all-gather.17.cloned.1.call-start = ((), (), s32[]{:S(2)}) async-start(), calls=%async_computation.4 | async-start | bytes 7864320 | tf_op jit(solution)/shard_map/all_gather | solution.py:408
  10.6 216.2 %all-gather.19.cloned.1.call-start = ((), (), s32[]{:S(2)}) async-start(), calls=%async_computation.5 | async-start | bytes 7864320 | tf_op jit(solution)/shard_map/all_gather | solution.py:408
  11.2 263.6 %all-gather.21.cloned.1.call-start = ((), (), s32[]{:S(2)}) async-start(), calls=%async_computation.6 | async-start | bytes 7864320 | tf_op jit(solution)/shard_map/all_gather | solution.py:408
  348.0 157.1 %collective-permute-start.45 = (bf16[2,768,1024]{2,1,0:T(8,128)(2,1)}, bf16[2,768,1024]{2,1,0:T(8,128)(2,1)}, u32[]{:S(2)}, u32[]{:S(2)}) collective-permute-start(bf16[2,768,1024]{2,1,0:T(8,128)(2,1)} %dynamic-slice_bitcast_fusion), channel_id=1, source_target_pairs={{0,1},{1,0},{2,3},{3,2},{4,5},{5,4},{6,7},{7,6},{8,9},{9,8},{10,11... | collective-permute-start | bytes 9437192 | tf_op jit(solution)/shard_map/ppermute | solution.py:348
  352.2 158.3 %collective-permute-start.37 = (bf16[2,256,3072]{2,1,0:T(8,128)(2,1)}, bf16[2,256,3072]{2,1,0:T(8,128)(2,1)}, u32[]{:S(2)}, u32[]{:S(2)}) collective-permute-start(bf16[2,256,3072]{2,1,0:T(8,128)(2,1)} %dynamic-slice_bitcast_fusion.1), channel_id=1, source_target_pairs={{0,1},{1,0},{2,3},{3,2},{4,5},{5,4},{6,7},{7,6},{8,9},{9,8},{10,11... | collective-permute-start | bytes 9437192 | tf_op jit(solution)/shard_map/ppermute | solution.py:348
  364.6 128.8 %collective-permute-start.21 = (bf16[2,512,1024]{2,1,0:T(8,128)(2,1)}, bf16[2,512,1024]{2,1,0:T(8,128)(2,1)}, u32[]{:S(2)}, u32[]{:S(2)}) collective-permute-start(bf16[2,512,1024]{2,1,0:T(8,128)(2,1)} %dynamic-slice_bitcast_fusion.3), channel_id=1, source_target_pairs={{0,1},{1,0},{2,3},{3,2},{4,5},{5,4},{6,7},{7,6},{8,9},{9,8},{10,11... | collective-permute-start | bytes 6291464 | tf_op jit(solution)/shard_map/ppermute | solution.py:348
  471.7 25.9 %collective-permute-start.13 = (bf16[2,256,2048]{2,1,0:T(8,128)(2,1)}, bf16[2,256,2048]{2,1,0:T(8,128)(2,1)}, u32[]{:S(2)}, u32[]{:S(2)}) collective-permute-start(bf16[2,256,2048]{2,1,0:T(8,128)(2,1)} %dynamic-slice_bitcast_fusion.4), channel_id=1, source_target_pairs={{0,1},{1,0},{2,3},{3,2},{4,5},{5,4},{6,7},{7,6},{8,9},{9,8},{10,11... | collective-permute-start | bytes 6291464 | tf_op jit(solution)/shard_map/ppermute | solution.py:348
  493.4 21.8 %collective-permute-start.29 = (bf16[2,256,3072]{2,1,0:T(8,128)(2,1)S(1)}, bf16[2,256,3072]{2,1,0:T(8,128)(2,1)}, u32[]{:S(2)}, u32[]{:S(2)}) collective-permute-start(bf16[2,256,3072]{2,1,0:T(8,128)(2,1)S(1)} %dynamic-slice_bitcast_fusion.2), channel_id=1, source_target_pairs={{0,1},{1,0},{2,3},{3,2},{4,5},{5,4},{6,7},{7,6},{8,9},{9,8},{10,11... | collective-permute-start | bytes 9437192 | tf_op jit(solution)/shard_map/ppermute | solution.py:348
  497.5 26.3 %collective-permute-start.22 = (bf16[512,1024]{1,0:T(8,128)(2,1)}, bf16[512,1024]{1,0:T(8,128)(2,1)}, u32[]{:S(2)}, u32[]{:S(2)}) collective-permute-start(bf16[512,1024]{1,0:T(8,128)(2,1)} %dynamic-slice_bitcast_fusion.9), channel_id=1, source_target_pairs={{0,2},{1,3},{2,0},{3,1},{4,6},{5,7},{6,4},{7,5},{8,10},{9,11},{10,... | collective-permute-start | bytes 3145736 | tf_op jit(solution)/shard_map/ppermute | solution.py:348
  501.6 44.7 %collective-permute-start.14 = (bf16[256,2048]{1,0:T(8,128)(2,1)}, bf16[256,2048]{1,0:T(8,128)(2,1)}, u32[]{:S(2)}, u32[]{:S(2)}) collective-permute-start(bf16[256,2048]{1,0:T(8,128)(2,1)} %dynamic-slice_bitcast_fusion.10), channel_id=1, source_target_pairs={{0,2},{1,3},{2,0},{3,1},{4,6},{5,7},{6,4},{7,5},{8,10},{9,11},{10,... | collective-permute-start | bytes 3145736 | tf_op jit(solution)/shard_map/ppermute | solution.py:348
  505.1 63.7 %collective-permute-start.6 = (bf16[256,2048]{1,0:T(8,128)(2,1)}, bf16[256,2048]{1,0:T(8,128)(2,1)}, u32[]{:S(2)}, u32[]{:S(2)}) collective-permute-start(bf16[256,2048]{1,0:T(8,128)(2,1)} %dynamic-slice_bitcast_fusion.11), channel_id=1, source_target_pairs={{0,2},{1,3},{2,0},{3,1},{4,6},{5,7},{6,4},{7,5},{8,10},{9,11},{10,... | collective-permute-start | bytes 3145736 | tf_op jit(solution)/shard_map/ppermute | solution.py:348
  510.5 132.1 %collective-permute-start.46 = (bf16[768,1024]{1,0:T(8,128)(2,1)}, bf16[768,1024]{1,0:T(8,128)(2,1)}, u32[]{:S(2)}, u32[]{:S(2)}) collective-permute-start(bf16[768,1024]{1,0:T(8,128)(2,1)} %dynamic-slice_bitcast_fusion.6), channel_id=1, source_target_pairs={{0,2},{1,3},{2,0},{3,1},{4,6},{5,7},{6,4},{7,5},{8,10},{9,11},{10,... | collective-permute-start | bytes 4718600 | tf_op jit(solution)/shard_map/ppermute | solution.py:348
  515.2 130.1 %collective-permute-start.38 = (bf16[256,3072]{1,0:T(8,128)(2,1)S(1)}, bf16[256,3072]{1,0:T(8,128)(2,1)S(1)}, u32[]{:S(2)}, u32[]{:S(2)}) collective-permute-start(bf16[256,3072]{1,0:T(8,128)(2,1)S(1)} %dynamic-slice_bitcast_fusion.7), channel_id=1, source_target_pairs={{0,2},{1,3},{2,0},{3,1},{4,6},{5,7},{6,4},{7,5},{8,10},{9,11},{10,... | collective-permute-start | bytes 4718600 | tf_op jit(solution)/shard_map/ppermute | solution.py:348
  523.9 145.0 %collective-permute-start.30 = (bf16[256,3072]{1,0:T(8,128)(2,1)S(1)}, bf16[256,3072]{1,0:T(8,128)(2,1)S(1)}, u32[]{:S(2)}, u32[]{:S(2)}) collective-permute-start(bf16[256,3072]{1,0:T(8,128)(2,1)S(1)} %dynamic-slice_bitcast_fusion.8), channel_id=1, source_target_pairs={{0,2},{1,3},{2,0},{3,1},{4,6},{5,7},{6,4},{7,5},{8,10},{9,11},{10,... | collective-permute-start | bytes 4718600 | tf_op jit(solution)/shard_map/ppermute | solution.py:348
  546.3 24.7 %collective-permute-start.23 = (bf16[2,2,64,1024]{3,2,0,1:T(8,128)(2,1)S(1)}, bf16[2,2,64,1024]{3,2,0,1:T(8,128)(2,1)S(1)}, u32[]{:S(2)}, u32[]{:S(2)}) collective-permute-start(bf16[2,2,64,1024]{3,2,0,1:T(8,128)(2,1)S(1)} %bitcast.347), channel_id=1, source_target_pairs={{0,4},{4,0},{8,12},{12,8},{16,20},{20,16},{24,28},{28,24},{1,5},{5... | collective-permute-start | bytes 1572872 | tf_op jit(solution)/shard_map/ppermute | solution.py:348
  636.9 37.1 %collective-permute-start.28 = (bf16[2,2,64,1024]{3,2,1,0:T(8,128)(2,1)S(1)}, bf16[2,2,64,1024]{3,2,1,0:T(8,128)(2,1)S(1)}, u32[]{:S(2)}, u32[]{:S(2)}) collective-permute-start(bf16[2,2,64,1024]{3,2,1,0:T(8,128)(2,1)S(1)} %pad_maximum_fusion.12), channel_id=1, source_target_pairs={{0,4},{4,0},{8,12},{12,8},{16,20},{20,16},{24,28},{28,24},{1,5},{5... | collective-permute-start | bytes 1572872 | tf_op jit(solution)/shard_map/ppermute | solution.py:348
  642.5 27.6 %collective-permute-start.20 = (bf16[2,2,32,2048]{3,2,1,0:T(8,128)(2,1)S(1)}, bf16[2,2,32,2048]{3,2,1,0:T(8,128)(2,1)S(1)}, u32[]{:S(2)}, u32[]{:S(2)}) collective-permute-start(bf16[2,2,32,2048]{3,2,1,0:T(8,128)(2,1)S(1)} %pad_maximum_fusion.11), channel_id=1, source_target_pairs={{0,8},{4,12},{8,0},{12,4},{16,24},{20,28},{24,16},{28,20},{1,9},{5... | collective-permute-start | bytes 1572872 | tf_op jit(solution)/shard_map/ppermute | solution.py:348
  642.6 29.5 %collective-permute-start.12 = (bf16[2,2,32,2048]{3,2,1,0:T(8,128)(2,1)S(1)}, bf16[2,2,32,2048]{3,2,1,0:T(8,128)(2,1)S(1)}, u32[]{:S(2)}, u32[]{:S(2)}) collective-permute-start(bf16[2,2,32,2048]{3,2,1,0:T(8,128)(2,1)S(1)} %pad_maximum_fusion.10), channel_id=1, source_target_pairs={{0,4},{4,0},{8,12},{12,8},{16,20},{20,16},{24,28},{28,24},{1,5},{5... | collective-permute-start | bytes 1572872 | tf_op jit(solution)/shard_map/ppermute | solution.py:348
  645.3 32.0 %collective-permute-start.47 = (bf16[2,2,96,1024]{3,2,1,0:T(8,128)(2,1)S(1)}, bf16[2,2,96,1024]{3,2,1,0:T(8,128)(2,1)S(1)}, u32[]{:S(2)}, u32[]{:S(2)}) collective-permute-start(bf16[2,2,96,1024]{3,2,1,0:T(8,128)(2,1)S(1)} %dynamic-slice_bitcast_fusion.12), channel_id=1, source_target_pairs={{0,8},{4,12},{8,0},{12,4},{16,24},{20,28},{24,16},{28,20},{1,9},{5... | collective-permute-start | bytes 2359304 | tf_op jit(solution)/shard_map/ppermute | solution.py:348
  668.9 27.0 %collective-permute-start.39 = (bf16[2,2,32,3072]{3,2,1,0:T(8,128)(2,1)S(1)}, bf16[2,2,32,3072]{3,2,1,0:T(8,128)(2,1)S(1)}, u32[]{:S(2)}, u32[]{:S(2)}) collective-permute-start(bf16[2,2,32,3072]{3,2,1,0:T(8,128)(2,1)S(1)} %dynamic-slice_bitcast_fusion.13), channel_id=1, source_target_pairs={{0,8},{4,12},{8,0},{12,4},{16,24},{20,28},{24,16},{28,20},{1,9},{5... | collective-permute-start | bytes 2359304 | tf_op jit(solution)/shard_map/ppermute | solution.py:348
  670.1 26.1 %collective-permute-start.31 = (bf16[2,2,32,3072]{3,2,0,1:T(8,128)(2,1)S(1)}, bf16[2,2,32,3072]{3,2,0,1:T(8,128)(2,1)S(1)}, u32[]{:S(2)}, u32[]{:S(2)}) collective-permute-start(bf16[2,2,32,3072]{3,2,0,1:T(8,128)(2,1)S(1)} %bitcast.346), channel_id=1, source_target_pairs={{0,4},{4,0},{8,12},{12,8},{16,20},{20,16},{24,28},{28,24},{1,5},{5... | collective-permute-start | bytes 2359304 | tf_op jit(solution)/shard_map/ppermute | solution.py:348
  727.0 28.6 %collective-permute-start.34 = (bf16[32,3072]{1,0:T(8,128)(2,1)S(1)}, bf16[32,3072]{1,0:T(8,128)(2,1)S(1)}, u32[]{:S(2)}, u32[]{:S(2)}) collective-permute-start(bf16[32,3072]{1,0:T(8,128)(2,1)S(1)} %fusion.37), channel_id=1, source_target_pairs={{0,16},{4,20},{8,24},{12,28},{16,0},{20,4},{24,8},{28,12},{1,17},{... | collective-permute-start | bytes 589832 | tf_op jit(solution)/shard_map/ppermute | solution.py:348
  727.1 36.9 %collective-permute-start.51 = (bf16[2,96,1024]{2,1,0:T(8,128)(2,1)S(1)}, bf16[2,96,1024]{2,1,0:T(8,128)(2,1)S(1)}, u32[]{:S(2)}, u32[]{:S(2)}) collective-permute-start(bf16[2,96,1024]{2,1,0:T(8,128)(2,1)S(1)} %pad_maximum_fusion.15), channel_id=1, source_target_pairs={{0,16},{4,20},{8,24},{12,28},{16,0},{20,4},{24,8},{28,12},{1,17},{... | collective-permute-start | bytes 1179656 | tf_op jit(solution)/shard_map/ppermute | solution.py:348
  730.2 42.2 %collective-permute-start.43 = (bf16[2,32,3072]{2,1,0:T(8,128)(2,1)S(1)}, bf16[2,32,3072]{2,1,0:T(8,128)(2,1)S(1)}, u32[]{:S(2)}, u32[]{:S(2)}) collective-permute-start(bf16[2,32,3072]{2,1,0:T(8,128)(2,1)S(1)} %pad_maximum_fusion.14), channel_id=1, source_target_pairs={{0,16},{4,20},{8,24},{12,28},{16,0},{20,4},{24,8},{28,12},{1,17},{... | collective-permute-start | bytes 1179656 | tf_op jit(solution)/shard_map/ppermute | solution.py:348
  755.6 25.2 %collective-permute-start.35 = (bf16[2,32,3072]{2,1,0:T(8,128)(2,1)S(1)}, bf16[2,32,3072]{2,1,0:T(8,128)(2,1)S(1)}, u32[]{:S(2)}, u32[]{:S(2)}) collective-permute-start(bf16[2,32,3072]{2,1,0:T(8,128)(2,1)S(1)} %pad_maximum_fusion.13), channel_id=1, source_target_pairs={{0,8},{4,12},{8,0},{12,4},{16,24},{20,28},{24,16},{28,20},{1,9},{5... | collective-permute-start | bytes 1179656 | tf_op jit(solution)/shard_map/ppermute | solution.py:348
  764.2 33.5 %collective-permute-start.52 = (bf16[2,2,96,1024]{3,2,1,0:T(8,128)(2,1)S(1)}, bf16[2,2,96,1024]{3,2,1,0:T(8,128)(2,1)S(1)}, u32[]{:S(2)}, u32[]{:S(2)}) collective-permute-start(bf16[2,2,96,1024]{3,2,1,0:T(8,128)(2,1)S(1)} %pad_maximum_fusion.9), channel_id=1, source_target_pairs={{0,8},{4,12},{8,0},{12,4},{16,24},{20,28},{24,16},{28,20},{1,9},{5... | collective-permute-start | bytes 2359304 | tf_op jit(solution)/shard_map/ppermute | solution.py:348
  772.6 41.9 %collective-permute-start.44 = (bf16[2,2,32,3072]{3,2,1,0:T(8,128)(2,1)S(1)}, bf16[2,2,32,3072]{3,2,1,0:T(8,128)(2,1)S(1)}, u32[]{:S(2)}, u32[]{:S(2)}) collective-permute-start(bf16[2,2,32,3072]{3,2,1,0:T(8,128)(2,1)S(1)} %pad_maximum_fusion.8), channel_id=1, source_target_pairs={{0,8},{4,12},{8,0},{12,4},{16,24},{20,28},{24,16},{28,20},{1,9},{5... | collective-permute-start | bytes 2359304 | tf_op jit(solution)/shard_map/ppermute | solution.py:348
  781.0 35.9 %collective-permute-start.36 = (bf16[2,2,32,3072]{3,2,1,0:T(8,128)(2,1)S(1)}, bf16[2,2,32,3072]{3,2,1,0:T(8,128)(2,1)S(1)}, u32[]{:S(2)}, u32[]{:S(2)}) collective-permute-start(bf16[2,2,32,3072]{3,2,1,0:T(8,128)(2,1)S(1)} %pad_maximum_fusion.7), channel_id=1, source_target_pairs={{0,4},{4,0},{8,12},{12,8},{16,20},{20,16},{24,28},{28,24},{1,5},{5... | collective-permute-start | bytes 2359304 | tf_op jit(solution)/shard_map/ppermute | solution.py:348
  (60 other events, 468.6 us)
Sparse Core Ops, SparseCore 0:
  9.6 25.3 all-gather.10
  36.5 22.6 all-gather.12
  60.7 34.4 all-gather.8
  96.7 34.4 all-gather.14
  132.6 46.3 all-gather.16
  180.4 46.3 all-gather.18
  228.4 46.3 all-gather.20
